TPU v7x, 32 devices: a whole 2x2x4 slice. The times are simulated.
32 devices in a mesh: dp: 4 (over y, core), expert: 8 (over z, x).
Axes of the slice: x: 2, y: 2, z: 4, core: 2. Of those that a mesh axis runs over, the one named last changes fastest.
Arguments:
- tokens: bfloat16 [384, 7168], P('expert'), may hold values from -6 to 6
- grad_out: bfloat16 [384, 7168], P('expert'), may hold values from -6 to 6
- routes: int32 [384, 2], P('expert'), may hold values from 0 to 7, all different within a row; in each aligned block of 48 rows (0 to 47, 48 to 95, ...) at most 15 rows name the same one
- gates: bfloat16 [384, 2], P('expert'), may hold values from 0.049804688 to 0.59765625
- w_gate: bfloat16 [8, 7168, 1024], P('expert', None, 'dp'), may hold values from -0.0625 to 0.0625
- w_up: bfloat16 [8, 7168, 1024], P('expert', None, 'dp'), may hold values from -0.0625 to 0.0625
- w_down: bfloat16 [8, 1024, 7168], P('expert', 'dp'), may hold values from -0.1875 to 0.1875
Outputs:
- grad_tokens: bfloat16 [384, 7168], P('expert', 'dp')
- grad_gates: float32 [384, 2], P('expert')
- grad_w_gate: bfloat16 [8, 7168, 1024], P('expert', None, 'dp')
- grad_w_up: bfloat16 [8, 7168, 1024], P('expert', None, 'dp')
- grad_w_down: bfloat16 [8, 1024, 7168], P('expert', 'dp')
Inputs may be any that keep to these rules, and one draw needn't show every extreme that they name: `routes`: within each aligned block of 48 tokens no expert is named by more than 15 pairs, a bound that some block reaches; the 2 experts of one token differ.
All inputs are finite; a program needn't handle non-finite values.
Results may differ from a plain program's by a relative error of at most 0.02.
Values may be sent and summed in bfloat16 or wider, within the bound.
A program may use at most 128 MiB of HBM per device.

v0:
```python
import jax
import jax.numpy as jnp
from jax import lax
from jax.sharding import PartitionSpec as P


def on_device(tokens, grad_out, routes, gates, w_gate, w_up, w_down):
    experts = lax.axis_size("expert")
    groups = lax.axis_size("dp")
    tok_rows = tokens.shape[0]
    width_full = tokens.shape[1]
    top = routes.shape[1]
    cap = tok_rows * top * 5 // (experts * 4)
    slots = experts * cap
    width = width_full // groups
    flat = routes.reshape(-1)
    onehot = (flat[:, None] == jnp.arange(experts, dtype=jnp.int32)[None, :]).astype(jnp.int32)
    earlier = jnp.cumsum(onehot, axis=0) - onehot
    position = jnp.sum(earlier * onehot, axis=1)
    slot_of = (flat * cap + position).reshape(tok_rows, top)
    match = slot_of[None, :, :] == jnp.arange(slots, dtype=jnp.int32)[:, None, None]
    place = jnp.any(match, axis=2).astype(jnp.bfloat16)
    gate_slots = jnp.sum(jnp.where(match, gates.astype(jnp.float32)[None, :, :], 0.0), axis=(1, 2))
    gate_slots = gate_slots.astype(jnp.bfloat16).reshape(experts, cap)

    def fill(source):
        filled = jnp.dot(place, source, preferred_element_type=jnp.float32).astype(jnp.bfloat16)
        return filled.reshape(experts, cap, source.shape[1])

    recv_in, recv_grad, recv_gate = (
        lax.all_to_all(fill(tokens), "expert", split_axis=0, concat_axis=0, tiled=True),
        lax.all_to_all(fill(grad_out), "expert", split_axis=0, concat_axis=0, tiled=True),
        lax.all_to_all(gate_slots, "expert", split_axis=0, concat_axis=0, tiled=True),
    )
    expert_in = recv_in.reshape(slots, width_full)
    expert_grad = recv_grad.reshape(slots, width_full)
    weight_col = recv_gate.reshape(slots).astype(jnp.float32)[:, None]
    gate_mat = w_gate[0]
    up_mat = w_up[0]
    down_mat = w_down[0]
    contract_last = (((1,), (1,)), ((), ()))
    contract_first = (((0,), (0,)), ((), ()))
    pre_gate = jnp.dot(expert_in, gate_mat, preferred_element_type=jnp.float32)
    pre_up = jnp.dot(expert_in, up_mat, preferred_element_type=jnp.float32)
    sigmoid_gate = jax.nn.sigmoid(pre_gate)
    activated = pre_gate * sigmoid_gate
    hidden = activated * pre_up
    stored = hidden.astype(jnp.bfloat16)
    back = lax.dot_general(expert_grad, down_mat, contract_last, preferred_element_type=jnp.float32)
    gate_terms = jnp.sum(stored.astype(jnp.float32) * back, axis=1)
    scaled = (weight_col * hidden).astype(jnp.bfloat16)
    grad_down = lax.dot_general(
        scaled, expert_grad, contract_first, preferred_element_type=jnp.float32
    ).astype(jnp.bfloat16)
    weighted = weight_col * back
    d_up = (weighted * activated).astype(jnp.bfloat16)
    d_gate = (weighted * pre_up * sigmoid_gate * (1.0 + pre_gate * (1.0 - sigmoid_gate))).astype(
        jnp.bfloat16
    )
    grad_gate = lax.dot_general(
        expert_in, d_gate, contract_first, preferred_element_type=jnp.float32
    ).astype(jnp.bfloat16)
    grad_up = lax.dot_general(
        expert_in, d_up, contract_first, preferred_element_type=jnp.float32
    ).astype(jnp.bfloat16)
    gate_total = lax.psum(gate_terms, "dp")
    first = lax.dot_general(gate_mat, d_gate, contract_last, preferred_element_type=jnp.float32)
    summed = lax.psum_scatter(
        (
            first + lax.dot_general(up_mat, d_up, contract_last, preferred_element_type=jnp.float32)
        ).astype(jnp.bfloat16),
        "dp",
        scatter_dimension=0,
        tiled=True,
    ).astype(jnp.float32)
    rows_back, gates_back = (
        lax.all_to_all(
            summed.reshape(width, experts, cap).astype(jnp.bfloat16),
            "expert",
            split_axis=1,
            concat_axis=1,
            tiled=True,
        ).astype(jnp.float32),
        lax.all_to_all(
            gate_total.reshape(1, experts, cap).astype(jnp.bfloat16),
            "expert",
            split_axis=1,
            concat_axis=1,
            tiled=True,
        ).astype(jnp.float32),
    )
    token_grad = lax.dot_general(
        place.astype(jnp.float32),
        rows_back.reshape(width, slots),
        (((0,), (1,)), ((), ())),
        precision=lax.Precision.HIGHEST,
        preferred_element_type=jnp.float32,
    )
    gate_flat = gates_back.reshape(slots)
    grad_gates = jnp.sum(jnp.where(match, gate_flat[:, None, None], 0.0), axis=0)
    return (
        token_grad.astype(jnp.bfloat16),
        grad_gates,
        grad_gate[None],
        grad_up[None],
        grad_down[None],
    )


def solution(mesh):
    placed = (
        P("expert", None),
        P("expert", None),
        P("expert", None),
        P("expert", None),
        P("expert", None, "dp"),
        P("expert", None, "dp"),
        P("expert", "dp", None),
    )
    return jax.shard_map(
        on_device,
        mesh=mesh,
        in_specs=placed,
        out_specs=(
            P("expert", "dp"),
            P("expert", None),
            P("expert", None, "dp"),
            P("expert", None, "dp"),
            P("expert", "dp", None),
        ),
        check_vma=False,
    )
```

profile of v0, /device:TPU:0, one launch (start us, length us, event | category | flops | bytes accessed | tf_op | source)
XLA Modules:
  0.0 203.4 jit_solution(7037050256204612789)
XLA Ops:
  10.2 1.8 reshape.77
  12.1 7.3 %all-to-all-start.2 = ((bf16[8,15,7168]{2,1,0:T(8,128)(2,1)}), bf16[8,15,7168]{2,1,0:T(8,128)(2,1)}, u32[]{:S(2)}, u32[]{:S(2)}) async-start(bf16[8,15,7168]{2,1,0:T(8,128)(2,1)} %reshape.77), calls=%async_computation.2 | async-start | bytes 3670016 | tf_op jit(solution)/shard_map/all_to_all | solution.py:31
  20.0 1.8 reshape.75
  21.8 40.2 %all-to-all-done.2 = bf16[8,15,7168]{2,1,0:T(8,128)(2,1)} async-done(((bf16[8,15,7168]{2,1,0:T(8,128)(2,1)}), bf16[8,15,7168]{2,1,0:T(8,128)(2,1)}, u32[]{:S(2)}, u32[]{:S(2)}) %all-to-all-start.2) | async-done | bytes 1720352 | tf_op jit(solution)/shard_map/all_to_all | solution.py:31
  62.0 4.3 %all-to-all-start.1 = ((bf16[8,15,7168]{2,1,0:T(8,128)(2,1)}), bf16[8,15,7168]{2,1,0:T(8,128)(2,1)}, u32[]{:S(2)}, u32[]{:S(2)}) async-start(bf16[8,15,7168]{2,1,0:T(8,128)(2,1)} %reshape.75), calls=%async_computation.1 | async-start | bytes 3670016 | tf_op jit(solution)/shard_map/all_to_all | solution.py:32
  66.3 2.1 %reshape.78 = bf16[120,7168]{1,0:T(8,128)(2,1)S(1)} reshape(bf16[8,15,7168]{2,1,0:T(8,128)(2,1)} %all-to-all-done.2) | data formatting | bytes 3440640 | tf_op jit(solution)/shard_map/reshape | solution.py:35
  68.5 2.8 %fusion.7 = f32[120,256]{1,0:T(8,128)S(1)} fusion(bf16[120,7168]{1,0:T(8,128)(2,1)S(1)} %reshape.78, bf16[1,7168,256]{2,1,0:T(8,128)(2,1)} %param.11), kind=kOutput, calls=%fused_computation.13 | convolution fusion | flops 440401920 | bytes 5513216 | tf_op jit(solution)/shard_map/dot_general | solution.py:43
  72.4 36.2 %all-to-all-done.1 = bf16[8,15,7168]{2,1,0:T(8,128)(2,1)} async-done(((bf16[8,15,7168]{2,1,0:T(8,128)(2,1)}), bf16[8,15,7168]{2,1,0:T(8,128)(2,1)}, u32[]{:S(2)}, u32[]{:S(2)}) %all-to-all-start.1) | async-done | bytes 1720352 | tf_op jit(solution)/shard_map/all_to_all | solution.py:32
  108.6 3.3 %reshape.76 = bf16[120,7168]{1,0:T(8,128)(2,1)} reshape(bf16[8,15,7168]{2,1,0:T(8,128)(2,1)} %all-to-all-done.1) | data formatting | bytes 3440640 | tf_op jit(solution)/shard_map/reshape | solution.py:36
  111.9 4.0 %multiply_reduce_fusion = (f32[120]{0:T(128)S(1)}, f32[120,256]{1,0:T(8,128)S(1)}) fusion(f32[120,256]{1,0:T(8,128)S(1)} %fusion.10, f32[120,256]{1,0:T(8,128)S(1)} %fusion.7, bf16[120,7168]{1,0:T(8,128)(2,1)} %reshape.76, bf16[1,256,7168]{2,1,0:T(8,128)(2,1)} %param.13), kind=kOutput, calls=%fused_computation.22 | convolution fusion | flops 440678272 | bytes 5759456 | tf_op jit(solution)/shard_map/dot_general | solution.py:49
  115.9 5.7 %psum.7 = bf16[120]{0:T(256)(128)(2,1)S(1)} all-reduce(f32[120]{0:T(128)S(1)} %get-tuple-element.9), channel_id=1, replica_groups=mesh['dp'=4,'expert'=8] {'dp'}, use_global_device_ids=true, to_apply=%region_6.7 | all-reduce | flops 120 | bytes 720 | tf_op jit(solution)/shard_map/psum | solution.py:66
  122.3 4.9 %all-to-all-start.4 = ((bf16[1,8,15]{2,0,1:T(2,128)(2,1)}), bf16[1,8,15]{2,0,1:T(2,128)(2,1)S(1)}, u32[]{:S(2)}, u32[]{:S(2)}) async-start(bf16[1,8,15]{2,0,1:T(2,128)(2,1)} %convert_element_type.116), calls=%async_computation.5 | async-start | bytes 8192 | tf_op jit(solution)/shard_map/all_to_all | solution.py:84
  127.2 6.3 %all-to-all-done.4 = bf16[1,8,15]{2,0,1:T(2,128)(2,1)S(1)} async-done(((bf16[1,8,15]{2,0,1:T(2,128)(2,1)}), bf16[1,8,15]{2,0,1:T(2,128)(2,1)S(1)}, u32[]{:S(2)}, u32[]{:S(2)}) %all-to-all-start.4) | async-done | bytes 272 | tf_op jit(solution)/shard_map/all_to_all | solution.py:84
  134.4 8.8 %all_to_all.26 = bf16[8,1,15]{2,1,0:T(2,128)(2,1)S(1)} all-to-all(bf16[8,1,15]{2,1,0:T(2,128)(2,1)S(1)} %convert_element_type.115), channel_id=1, replica_groups=mesh['dp'=4,'expert'=8] {'expert'}, dimensions={0} | all-to-all | bytes 480 | tf_op jit(solution)/shard_map/all_to_all | solution.py:33
  143.5 3.4 %fusion.5 = f32[120,7168]{1,0:T(8,128)S(1)} fusion(bf16[120,256]{1,0:T(8,128)(2,1)S(1)} %get-tuple-element.8, bf16[1,7168,256]{2,1,0:T(8,128)(2,1)} %param.11), kind=kOutput, calls=%fused_computation.11 | convolution fusion | flops 440401920 | bytes 7172096 | tf_op jit(solution)/shard_map/dot_general | solution.py:67
  147.0 2.5 %fusion.4 = bf16[7168,120]{0,1:T(8,128)(2,1)} fusion(f32[120,7168]{1,0:T(8,128)S(1)} %fusion.5, bf16[120,256]{1,0:T(8,128)(2,1)S(1)} %get-tuple-element.7, bf16[1,7168,256]{2,1,0:T(8,128)(2,1)S(1)} %copy-done.2), kind=kOutput, calls=%fused_computation.10 | convolution fusion | flops 442122240 | bytes 8892416 | tf_op jit(solution)/shard_map/dot_general | solution.py:70
  149.5 25.6 %reduce-scatter.2.cloned.1.call-done = bf16[1792,120]{0,1:T(8,128)(2,1)} async-done(((bf16[7168,120]{0,1:T(8,128)(2,1)}), bf16[1792,120]{0,1:T(8,128)(2,1)}) %reduce-scatter.2.cloned.1.call-update) | async-done | bytes 430096 | tf_op jit(solution)/shard_map/reduce_scatter | solution.py:68
  175.1 1.9 convert_element_type.104
  177.0 5.5 %all-to-all-start.3 = ((bf16[1792,8,15]{0,2,1:T(8,128)(2,1)}), bf16[1792,8,15]{0,2,1:T(8,128)(2,1)S(1)}, u32[]{:S(2)}, u32[]{:S(2)}) async-start(bf16[1792,8,15]{0,2,1:T(8,128)(2,1)} %convert_element_type.104), calls=%async_computation.4 | async-start | bytes 917504 | tf_op jit(solution)/shard_map/all_to_all | solution.py:77
  182.5 4.5 %fusion.2 = bf16[1,256,7168]{2,1,0:T(8,128)(2,1)} fusion(bf16[120,7168]{1,0:T(8,128)(2,1)} %reshape.76, f32[120]{0:T(128)S(1)} %reshape.80, f32[120,256]{1,0:T(8,128)S(1)} %fusion.10, f32[120,256]{1,0:T(8,128)S(1)} %fusion.7), kind=kOutput, calls=%fused_computation.5 | convolution fusion | flops 442451968 | bytes 5636576 | tf_op jit(solution)/shard_map/dot_general | solution.py:52
  187.0 3.0 %fusion.1 = bf16[1,7168,256]{2,1,0:T(8,128)(2,1)} fusion(bf16[120,7168]{1,0:T(8,128)(2,1)S(1)} %reshape.78, bf16[120,256]{1,0:T(8,128)(2,1)S(1)} %get-tuple-element.7), kind=kOutput, calls=%fused_computation.4 | convolution fusion | flops 442236928 | bytes 5451776 | tf_op jit(solution)/shard_map/dot_general | solution.py:63
  190.0 3.0 %fusion = bf16[1,7168,256]{2,1,0:T(8,128)(2,1)} fusion(bf16[120,7168]{1,0:T(8,128)(2,1)S(1)} %reshape.78, bf16[120,256]{1,0:T(8,128)(2,1)S(1)} %get-tuple-element.8), kind=kOutput, calls=%fused_computation.3 | convolution fusion | flops 442236928 | bytes 5451776 | tf_op jit(solution)/shard_map/dot_general | solution.py:60
  193.0 2.6 %all-to-all-done.3 = bf16[1792,8,15]{0,2,1:T(8,128)(2,1)S(1)} async-done(((bf16[1792,8,15]{0,2,1:T(8,128)(2,1)}), bf16[1792,8,15]{0,2,1:T(8,128)(2,1)S(1)}, u32[]{:S(2)}, u32[]{:S(2)}) %all-to-all-start.3) | async-done | bytes 430112 | tf_op jit(solution)/shard_map/all_to_all | solution.py:77
  195.7 0.9 convolution_convert_fusion.5
  (34 shorter events, 6.7 us)
Async XLA Ops:
  7.2 2.4 %copy-start = (bf16[48,7168]{1,0:T(8,128)(2,1)S(1)}, bf16[48,7168]{1,0:T(8,128)(2,1)}, u32[]{:S(2)}) copy-start(bf16[48,7168]{1,0:T(8,128)(2,1)} %param.7) | copy-start | bytes 2064388
  10.2 9.1 %copy-start.3 = (bf16[48,7168]{1,0:T(8,128)(2,1)S(1)}, bf16[48,7168]{1,0:T(8,128)(2,1)}, u32[]{:S(2)}) copy-start(bf16[48,7168]{1,0:T(8,128)(2,1)} %param.8) | copy-start | bytes 2064388
  12.1 50.0 %all-to-all-start.2 = ((bf16[8,15,7168]{2,1,0:T(8,128)(2,1)}), bf16[8,15,7168]{2,1,0:T(8,128)(2,1)}, u32[]{:S(2)}, u32[]{:S(2)}) async-start(bf16[8,15,7168]{2,1,0:T(8,128)(2,1)} %reshape.77), calls=%async_computation.2 | async-start | bytes 3670016 | tf_op jit(solution)/shard_map/all_to_all | solution.py:31
  62.0 46.6 %all-to-all-start.1 = ((bf16[8,15,7168]{2,1,0:T(8,128)(2,1)}), bf16[8,15,7168]{2,1,0:T(8,128)(2,1)}, u32[]{:S(2)}, u32[]{:S(2)}) async-start(bf16[8,15,7168]{2,1,0:T(8,128)(2,1)} %reshape.75), calls=%async_computation.1 | async-start | bytes 3670016 | tf_op jit(solution)/shard_map/all_to_all | solution.py:32
  68.5 3.1 %copy-start.1 = (bf16[1,7168,256]{2,1,0:T(8,128)(2,1)S(1)}, bf16[1,7168,256]{2,1,0:T(8,128)(2,1)}, u32[]{:S(2)}) copy-start(bf16[1,7168,256]{2,1,0:T(8,128)(2,1)} %param.12) | copy-start | bytes 11010052
  111.9 15.3 %copy-start.4 = (bf16[48,2]{0,1:T(2,128)(2,1)S(1)}, bf16[48,2]{0,1:T(2,128)(2,1)}, u32[]{:S(2)}) copy-start(bf16[48,2]{0,1:T(2,128)(2,1)} %param.10) | copy-start | bytes 580
  122.3 11.2 %all-to-all-start.4 = ((bf16[1,8,15]{2,0,1:T(2,128)(2,1)}), bf16[1,8,15]{2,0,1:T(2,128)(2,1)S(1)}, u32[]{:S(2)}, u32[]{:S(2)}) async-start(bf16[1,8,15]{2,0,1:T(2,128)(2,1)} %convert_element_type.116), calls=%async_computation.5 | async-start | bytes 8192 | tf_op jit(solution)/shard_map/all_to_all | solution.py:84
  127.1 47.9 %reduce-scatter.2.cloned.1.call-start = ((), (), s32[]{:S(2)}) async-start(), calls=%async_computation.6 | async-start | bytes 2150400 | tf_op jit(solution)/shard_map/reduce_scatter | solution.py:68
  143.5 3.5 %copy-start.2 = (bf16[1,7168,256]{2,1,0:T(8,128)(2,1)S(1)}, bf16[1,7168,256]{2,1,0:T(8,128)(2,1)}, u32[]{:S(2)}) copy-start(bf16[1,7168,256]{2,1,0:T(8,128)(2,1)} %param.12) | copy-start | bytes 11010052
  177.0 18.6 %all-to-all-start.3 = ((bf16[1792,8,15]{0,2,1:T(8,128)(2,1)}), bf16[1792,8,15]{0,2,1:T(8,128)(2,1)S(1)}, u32[]{:S(2)}, u32[]{:S(2)}) async-start(bf16[1792,8,15]{0,2,1:T(8,128)(2,1)} %convert_element_type.104), calls=%async_computation.4 | async-start | bytes 917504 | tf_op jit(solution)/shard_map/all_to_all | solution.py:77
Sparse Core Ops, SparseCore 0:
  149.6 25.4 reduce-scatter.1
where the time goes:
time: 204 us; the launch traced here: 203 us
  waiting for transfers between devices  111 us (54%)
  matrix products  26.2 us (13%)
  starting transfers between devices  22 us (11%)
  blocking collectives  14.5 us (7%)
  between operations  14.2 us (7%)
  local copies, waits for them, and re-layouts  13.6 us (7%)
  other arithmetic  2.05 us (1%)
    all_to_all x1, waiting for transfers between devices, on_device(): lax.all_to_all(fill(tokens), 'expert', split_axis=0, concat_axis=0, tiled...  40.2 us
    all_to_all x1, waiting for transfers between devices, on_device(): lax.all_to_all(fill(grad_out), 'expert', split_axis=0, concat_axis=0, til...  36.2 us
    reduce_scatter x1, waiting for transfers between devices, on_device(): lax.psum_scatter((first + lax.dot_general(up_mat, d_up, contract_last, pr...  25.6 us
    all_to_all x1, blocking collectives, on_device(): lax.all_to_all(gate_slots, 'expert', split_axis=0, concat_axis=0, tiled=T...  8.82 us
    all_to_all x1, starting transfers between devices, on_device(): lax.all_to_all(fill(tokens), 'expert', split_axis=0, concat_axis=0, tiled...  7.25 us
    all_to_all x1, waiting for transfers between devices, on_device(): lax.all_to_all(gate_total.reshape(1, experts, cap).astype(jnp.bfloat16),...  6.32 us
    psum x1, blocking collectives, on_device(): gate_total = lax.psum(gate_terms, 'dp')  5.68 us
    all_to_all x1, starting transfers between devices, on_device(): lax.all_to_all(summed.reshape(width, experts, cap).astype(jnp.bfloat16),...  5.51 us
  transfers between devices with their start and end apart: 5, of which 5 were waited for; matrix products, arithmetic and copies ran while one was open for 9% of the time, Pallas kernels for 0%

commit v1 on v0

v1 whole, which is shorter than its diff:
```python
import jax
import jax.numpy as jnp
from jax import lax
from jax.sharding import PartitionSpec as P

CONTRACT_LAST = (((1,), (1,)), ((), ()))
CONTRACT_FIRST = (((0,), (0,)), ((), ()))
LANES = 128
ROWS = 16


def on_device(tokens, grad_out, routes, gates, w_gate, w_up, w_down):
    experts = lax.axis_size("expert")
    groups = lax.axis_size("dp")
    part = lax.axis_index("dp")
    tok_rows, width_full = tokens.shape
    top = routes.shape[1]
    cap = tok_rows * top * 5 // (experts * 4)
    room = (cap + ROWS - 1) // ROWS * ROWS
    slots = experts * room
    width = width_full // groups
    flat = routes.reshape(-1)
    pair = jnp.arange(flat.shape[0], dtype=jnp.int32)
    earlier = (flat[:, None] == flat[None, :]) & (pair[None, :] < pair[:, None])
    position = jnp.sum(earlier.astype(jnp.int32), axis=1)
    slot_of = (flat * room + position).reshape(tok_rows, top)
    match = slot_of[None, :, :] == jnp.arange(slots, dtype=jnp.int32)[:, None, None]
    place = jnp.any(match, axis=2).astype(jnp.bfloat16)
    gate_slots = jnp.sum(jnp.where(match, gates.astype(jnp.float32)[None, :, :], 0.0), axis=(1, 2))
    gate_slots = gate_slots.astype(jnp.bfloat16)

    def fill(source):
        share = lax.dynamic_slice_in_dim(source, part * width, width, axis=1)
        return jnp.dot(place, share, preferred_element_type=jnp.float32).astype(jnp.bfloat16)

    def swap(sent):
        swapped = lax.all_to_all(
            sent.reshape(experts, room, sent.shape[1]), "expert", split_axis=0, concat_axis=0, tiled=True
        )
        return swapped.reshape(slots, sent.shape[1])

    def join(shares):
        whole = lax.all_gather(shares, "dp", axis=0)
        return whole.transpose(1, 0, 2).reshape(slots, width_full)

    expert_in = join(swap(fill(tokens)))
    weight_lanes = jnp.pad(gate_slots[:, None], ((0, 0), (0, LANES - 1)))
    recv_grad = swap(jnp.concatenate([fill(grad_out), weight_lanes], axis=1))
    expert_grad = join(recv_grad[:, :width])
    weight_col = recv_grad[:, width : width + 1].astype(jnp.float32)
    gate_mat = w_gate[0]
    up_mat = w_up[0]
    down_mat = w_down[0]
    pre_gate = jnp.dot(expert_in, gate_mat, preferred_element_type=jnp.float32)
    pre_up = jnp.dot(expert_in, up_mat, preferred_element_type=jnp.float32)
    sigmoid_gate = jax.nn.sigmoid(pre_gate)
    activated = pre_gate * sigmoid_gate
    hidden = activated * pre_up
    stored = hidden.astype(jnp.bfloat16)
    back = lax.dot_general(expert_grad, down_mat, CONTRACT_LAST, preferred_element_type=jnp.float32)
    gate_terms = jnp.sum(stored.astype(jnp.float32) * back, axis=1)
    scaled = (weight_col * hidden).astype(jnp.bfloat16)
    grad_down = lax.dot_general(
        scaled, expert_grad, CONTRACT_FIRST, preferred_element_type=jnp.float32
    ).astype(jnp.bfloat16)
    weighted = weight_col * back
    d_up = (weighted * activated).astype(jnp.bfloat16)
    d_gate = (weighted * pre_up * sigmoid_gate * (1.0 + pre_gate * (1.0 - sigmoid_gate))).astype(
        jnp.bfloat16
    )
    grad_gate = lax.dot_general(
        expert_in, d_gate, CONTRACT_FIRST, preferred_element_type=jnp.float32
    ).astype(jnp.bfloat16)
    grad_up = lax.dot_general(
        expert_in, d_up, CONTRACT_FIRST, preferred_element_type=jnp.float32
    ).astype(jnp.bfloat16)
    high = gate_terms.astype(jnp.bfloat16)
    low = (gate_terms - high.astype(jnp.float32)).astype(jnp.bfloat16)
    term_lanes = jnp.pad(jnp.stack([high, low], axis=1), ((0, 0), (0, LANES - 2)))

    def block(n):
        rows = slice(n * width, (n + 1) * width)
        first = lax.dot_general(d_gate, gate_mat[rows], CONTRACT_LAST, preferred_element_type=jnp.float32)
        second = lax.dot_general(d_up, up_mat[rows], CONTRACT_LAST, preferred_element_type=jnp.float32)
        return jnp.concatenate([(first + second).astype(jnp.bfloat16), term_lanes], axis=1)

    blocks = jnp.concatenate([block(n) for n in range(groups)], axis=0)
    summed = lax.psum_scatter(blocks, "dp", scatter_dimension=0, tiled=True)
    back_home = swap(summed)
    token_grad = lax.dot_general(
        place, back_home[:, :width], CONTRACT_FIRST, preferred_element_type=jnp.float32
    )
    gate_flat = jnp.sum(back_home[:, width : width + 2].astype(jnp.float32), axis=1)
    grad_gates = jnp.sum(jnp.where(match, gate_flat[:, None, None], 0.0), axis=0)
    return (
        token_grad.astype(jnp.bfloat16),
        grad_gates,
        grad_gate[None],
        grad_up[None],
        grad_down[None],
    )


def solution(mesh):
    placed = (
        P("expert", None),
        P("expert", None),
        P("expert", None),
        P("expert", None),
        P("expert", None, "dp"),
        P("expert", None, "dp"),
        P("expert", "dp", None),
    )
    return jax.shard_map(
        on_device,
        mesh=mesh,
        in_specs=placed,
        out_specs=(
            P("expert", "dp"),
            P("expert", None),
            P("expert", None, "dp"),
            P("expert", None, "dp"),
            P("expert", "dp", None),
        ),
        check_vma=False,
    )
```

time: 204 us -> 158 us (0.77)
  waiting for transfers between devices: 111 us -> 53.4 us
  blocking collectives: 14.5 us -> 37.2 us
  starting transfers between devices: 22 us -> 5.74 us
  other arithmetic: 2.05 us -> 8.66 us
  local copies, waits for them, and re-layouts: 13.6 us -> 9.63 us
  matrix products: 26.2 us -> 29.2 us
    all_to_all x4 -> x1, waiting for transfers between devices: 85.4 us -> 4.86 us  [swap(): lax.all_to_all(sent.reshape(experts, room, sent.shape[1]), 'expert', spli...]
    all_to_all x1 -> x2, blocking collectives: 8.82 us -> 37.2 us  [swap(): lax.all_to_all(sent.reshape(experts, room, sent.shape[1]), 'expert', spli...]
    all_gather x0 -> x2, waiting for transfers between devices: none -> 17.7 us  [join(): whole = lax.all_gather(shares, 'dp', axis=0)]
    all_to_all x4 -> x1, starting transfers between devices: 21.9 us -> 5.62 us  [swap(): lax.all_to_all(sent.reshape(experts, room, sent.shape[1]), 'expert', spli...]
    reshape x5 -> x0, local copies, waits for them, and re-layouts: 9.27 us -> none  [the longest x2 3.68 us: fill(): return filled.reshape(experts, cap, source.shape[1])]
    all_gather x0 -> x2, local copies, waits for them, and re-layouts: none -> 6.71 us  [join(): whole = lax.all_gather(shares, 'dp', axis=0)]
    psum x1 -> x0, blocking collectives: 5.68 us -> none  [on_device(): gate_total = lax.psum(gate_terms, 'dp')]
    concatenate x0 -> x2, other arithmetic: none -> 5.48 us  [the longest x1 5.44 us: on_device(): blocks = jnp.concatenate([block(n) for n in range(groups)], axis=0)]
  transfers between devices with their start and end apart: 5 -> 4, of which waited for: 5 -> 4; matrix products, arithmetic and copies ran while one was open for 9% -> 11% of each run, Pallas kernels for 0% -> 0%
where the time goes in v1:
time: 158 us
  waiting for transfers between devices  53.4 us (34%)
  blocking collectives  37.2 us (24%)
  matrix products  29.2 us (18%)
  between operations  13.9 us (9%)
  local copies, waits for them, and re-layouts  9.63 us (6%)
  other arithmetic  8.66 us (5%)
  starting transfers between devices  5.74 us (4%)
    all_to_all x2, blocking collectives, swap(): lax.all_to_all(sent.reshape(experts, room, sent.shape[1]), 'expert', spli...  37.2 us
    reduce_scatter x1, waiting for transfers between devices, on_device(): summed = lax.psum_scatter(blocks, 'dp', scatter_dimension=0, tiled=True)  30.8 us
    all_gather x2, waiting for transfers between devices, join(): whole = lax.all_gather(shares, 'dp', axis=0)  17.7 us
    all_gather x2, local copies, waits for them, and re-layouts, join(): whole = lax.all_gather(shares, 'dp', axis=0)  6.71 us
    all_to_all x1, starting transfers between devices, swap(): lax.all_to_all(sent.reshape(experts, room, sent.shape[1]), 'expert', spli...  5.62 us
    concatenate x1, other arithmetic, on_device(): blocks = jnp.concatenate([block(n) for n in range(groups)], axis=0)  5.44 us
    dot_general x4, matrix products, block(): lax.dot_general(d_up, up_mat[rows], CONTRACT_LAST, preferred_element_type...  4.91 us
    all_to_all x1, waiting for transfers between devices, swap(): lax.all_to_all(sent.reshape(experts, room, sent.shape[1]), 'expert', spli...  4.86 us
  transfers between devices with their start and end apart: 4, of which 4 were waited for; matrix products, arithmetic and copies ran while one was open for 11% of the time, Pallas kernels for 0%

profile of v1, /device:TPU:0, one launch (start us, length us, event | category | flops | bytes accessed | tf_op | source)
XLA Modules:
  0.0 157.8 jit_solution(9177184004251885102)
XLA Ops:
  7.2 0.8 copy.54
  9.7 20.4 %all_to_all.15 = bf16[8,16,1792]{2,1,0:T(8,128)(2,1)} all-to-all(bf16[8,16,1792]{2,1,0:T(8,128)(2,1)S(1)} %bitcast.96), channel_id=1, replica_groups=mesh['dp'=4,'expert'=8] {'expert'}, dimensions={0} | all-to-all | bytes 917504 | tf_op jit(solution)/shard_map/all_to_all | solution.py:37
  31.1 1.3 convolution_convert_fusion.4
  32.4 16.8 %all_to_all.16 = bf16[8,16,1920]{2,1,0:T(8,128)(2,1)S(1)} all-to-all(bf16[8,16,1920]{2,1,0:T(8,128)(2,1)S(1)} %bitcast.93), channel_id=1, replica_groups=mesh['dp'=4,'expert'=8] {'expert'}, dimensions={0} | all-to-all | bytes 983040 | tf_op jit(solution)/shard_map/all_to_all | solution.py:37
  49.2 0.8 slice.81
  50.3 2.9 %copy.58 = bf16[4,128,1792]{1,2,0:T(8,128)(2,1)S(1)} copy(bf16[4,128,1792]{2,1,0:T(8,128)(2,1)} %all-gather.4.cloned.1.call-done) | data formatting | bytes 3670016 | tf_op jit(solution)/shard_map/all_gather | solution.py:43
  53.2 2.8 %fusion.5 = f32[128,256]{1,0:T(8,128)S(1)} fusion(bf16[128,7168]{0,1:T(8,128)(2,1)S(1)} %bitcast.83, bf16[1,7168,256]{2,1,0:T(8,128)(2,1)} %param.12), kind=kOutput, calls=%fused_computation.8 | convolution fusion | flops 469762048 | bytes 5636096 | tf_op jit(solution)/shard_map/dot_general | solution.py:55
  56.0 17.6 %all-gather.6.cloned.1.call-done = bf16[512,1792]{1,0:T(8,128)(2,1)} async-done(((bf16[128,1792]{1,0:T(8,128)(2,1)}), bf16[512,1792]{1,0:T(8,128)(2,1)}) %all-gather.6.cloned.1.call-update) | async-done | bytes 1835024 | tf_op jit(solution)/shard_map/all_gather | solution.py:43
  73.6 3.8 %copy.57 = bf16[4,128,1792]{1,2,0:T(8,128)(2,1)} copy(bf16[4,128,1792]{2,1,0:T(8,128)(2,1)} %bitcast.94) | data formatting | bytes 3670016 | tf_op jit(solution)/shard_map/all_gather | solution.py:43
  77.4 4.1 %fusion.7 = f32[128,256]{1,0:T(8,128)S(1)} fusion(bf16[128,7168]{0,1:T(8,128)(2,1)} %bitcast.87, bf16[1,256,7168]{2,1,0:T(8,128)(2,1)} %param.13), kind=kOutput, calls=%fused_computation.10 | convolution fusion | flops 469762048 | bytes 5636096 | tf_op jit(solution)/shard_map/dot_general | solution.py:60
  81.5 1.5 multiply_convert_fusion.2
  83.0 1.4 fusion.15
  84.4 1.4 fusion.18
  85.8 1.4 fusion.21
  89.0 2.1 %fusion.12 = bf16[128,1792]{1,0:T(8,128)(2,1)S(1)} fusion(f32[128,1792]{1,0:T(8,128)} %fusion.15, bf16[128,256]{1,0:T(8,128)(2,1)S(1)} %get-tuple-element.7, bf16[1,7168,256]{2,1,0:T(8,128)(2,1)} %param.12), kind=kOutput, calls=%fused_computation.19 | convolution fusion | flops 117899264 | bytes 2359296 | tf_op jit(solution)/shard_map/dot_general | solution.py:84
  91.0 1.9 %fusion.11 = bf16[128,1792]{1,0:T(8,128)(2,1)S(1)} fusion(f32[128,1792]{1,0:T(8,128)} %fusion.18, bf16[128,256]{1,0:T(8,128)(2,1)S(1)} %get-tuple-element.7, bf16[1,7168,256]{2,1,0:T(8,128)(2,1)} %param.12), kind=kOutput, calls=%fused_computation.18 | convolution fusion | flops 117899264 | bytes 2359296 | tf_op jit(solution)/shard_map/dot_general | solution.py:84
  93.9 5.4 %maximum_maximum_fusion = bf16[512,1920]{1,0:T(8,128)(2,1)} fusion(bf16[128,128]{1,0:T(8,128)(2,1)S(1)} %pad.9, bf16[128,1792]{1,0:T(8,128)(2,1)S(1)} %fusion.12, bf16[128,1792]{1,0:T(8,128)(2,1)S(1)} %fusion.11, bf16[128,1792]{1,0:T(8,128)(2,1)S(1)} %fusion.10, bf16[128,1792]{1,0:T(8,128)(2,1)S(1)} %fusion.9), kind=kLoop, calls=%fused_computation.23 | loop fusion | flops 15728640 | bytes 3833856 | tf_op jit(solution)/shard_map/concatenate | solution.py:87
  99.4 30.8 %reduce-scatter.2.cloned.1.call-done = bf16[128,1920]{1,0:T(8,128)(2,1)} async-done(((bf16[512,1920]{1,0:T(8,128)(2,1)}), bf16[128,1920]{1,0:T(8,128)(2,1)}) %reduce-scatter.2.cloned.1.call-update) | async-done | bytes 491536 | tf_op jit(solution)/shard_map/reduce_scatter | solution.py:88
  130.2 5.6 %all-to-all-start.2 = ((bf16[8,16,1920]{2,1,0:T(8,128)(2,1)}), bf16[8,16,1920]{2,1,0:T(8,128)(2,1)S(1)}, u32[]{:S(2)}, u32[]{:S(2)}) async-start(bf16[8,16,1920]{2,1,0:T(8,128)(2,1)} %bitcast.97), calls=%async_computation.3 | async-start | bytes 983040 | tf_op jit(solution)/shard_map/all_to_all | solution.py:37
  135.8 2.9 %fusion.1 = bf16[1,7168,256]{2,1,0:T(8,128)(2,1)} fusion(bf16[128,7168]{0,1:T(8,128)(2,1)S(1)} %bitcast.85, bf16[128,256]{1,0:T(8,128)(2,1)S(1)} %get-tuple-element.7), kind=kOutput, calls=%fused_computation.4 | convolution fusion | flops 471597056 | bytes 5570560 | tf_op jit(solution)/shard_map/dot_general | solution.py:74
  138.7 2.9 %fusion = bf16[1,7168,256]{2,1,0:T(8,128)(2,1)} fusion(bf16[128,7168]{0,1:T(8,128)(2,1)S(1)} %bitcast.86, bf16[128,256]{1,0:T(8,128)(2,1)S(1)} %copy-done.6), kind=kOutput, calls=%fused_computation.3 | convolution fusion | flops 471597056 | bytes 5570560 | tf_op jit(solution)/shard_map/dot_general | solution.py:71
  141.7 3.1 %fusion.2 = bf16[1,256,7168]{2,1,0:T(8,128)(2,1)} fusion(bf16[128,7168]{0,1:T(8,128)(2,1)S(1)} %bitcast.88, f32[128]{0:T(128)S(1)} %convert_reduce_fusion, f32[128,256]{1,0:T(8,128)S(1)} %copy-done.8, f32[128,256]{1,0:T(8,128)S(1)} %copy-done.9), kind=kOutput, calls=%fused_computation.5 | convolution fusion | flops 471826432 | bytes 5767680 | tf_op jit(solution)/shard_map/dot_general | solution.py:63
  144.7 4.9 %all-to-all-done.2 = bf16[8,16,1920]{2,1,0:T(8,128)(2,1)S(1)} async-done(((bf16[8,16,1920]{2,1,0:T(8,128)(2,1)}), bf16[8,16,1920]{2,1,0:T(8,128)(2,1)S(1)}, u32[]{:S(2)}, u32[]{:S(2)}) %all-to-all-start.2) | async-done | bytes 491552 | tf_op jit(solution)/shard_map/all_to_all | solution.py:37
  149.7 0.9 convolution_convert_fusion.5
  (49 shorter events, 6.5 us)
Async XLA Ops:
  7.2 2.2 %copy-start = (bf16[48,7168]{1,0:T(8,128)(2,1)S(1)}, bf16[48,7168]{1,0:T(8,128)(2,1)}, u32[]{:S(2)}) copy-start(bf16[48,7168]{1,0:T(8,128)(2,1)} %param.7) | copy-start | bytes 2064388
  7.2 43.1 %all-gather.4.cloned.1.call-start = ((), (), s32[]{:S(2)}) async-start(), calls=%async_computation.4 | async-start | bytes 2293760 | tf_op jit(solution)/shard_map/all_gather | solution.py:43
  30.1 43.5 %all-gather.6.cloned.1.call-start = ((), (), s32[]{:S(2)}) async-start(), calls=%async_computation.6 | async-start | bytes 2293760 | tf_op jit(solution)/shard_map/all_gather | solution.py:43
  50.0 80.1 %reduce-scatter.2.cloned.1.call-start = ((), (), s32[]{:S(2)}) async-start(), calls=%async_computation.5 | async-start | bytes 2457600 | tf_op jit(solution)/shard_map/reduce_scatter | solution.py:88
  56.0 25.5 %copy-start.7 = (f32[128,256]{1,0:T(8,128)}, f32[128,256]{1,0:T(8,128)S(1)}, u32[]{:S(2)}) copy-start(f32[128,256]{1,0:T(8,128)S(1)} %fusion.5) | copy-start | bytes 393220
  77.4 4.1 %copy-start.3 = (bf16[1,7168,256]{2,1,0:T(8,128)(2,1)S(1)}, bf16[1,7168,256]{2,1,0:T(8,128)(2,1)}, u32[]{:S(2)}) copy-start(bf16[1,7168,256]{2,1,0:T(8,128)(2,1)} %param.11) | copy-start | bytes 11010052
  83.0 4.6 %copy-start.5 = (bf16[128,256]{1,0:T(8,128)(2,1)}, bf16[128,256]{1,0:T(8,128)(2,1)S(1)}, u32[]{:S(2)}) copy-start(bf16[128,256]{1,0:T(8,128)(2,1)S(1)} %get-tuple-element.5) | copy-start | bytes 196612
  89.0 4.0 %copy-start.2 = (bf16[1,7168,256]{2,1,0:T(8,128)(2,1)S(1)}, bf16[1,7168,256]{2,1,0:T(8,128)(2,1)}, u32[]{:S(2)}) copy-start(bf16[1,7168,256]{2,1,0:T(8,128)(2,1)} %param.12) | copy-start | bytes 11010052
  89.0 4.0 %copy-start.4 = (f32[128,1792]{1,0:T(8,128)S(1)}, f32[128,1792]{1,0:T(8,128)}, u32[]{:S(2)}) copy-start(f32[128,1792]{1,0:T(8,128)} %fusion.21) | copy-start | bytes 2752516
  130.2 8.6 %copy-start.6 = (bf16[128,256]{1,0:T(8,128)(2,1)S(1)}, bf16[128,256]{1,0:T(8,128)(2,1)}, u32[]{:S(2)}) copy-start(bf16[128,256]{1,0:T(8,128)(2,1)} %copy-done.5) | copy-start | bytes 196612
  130.2 19.4 %all-to-all-start.2 = ((bf16[8,16,1920]{2,1,0:T(8,128)(2,1)}), bf16[8,16,1920]{2,1,0:T(8,128)(2,1)S(1)}, u32[]{:S(2)}, u32[]{:S(2)}) async-start(bf16[8,16,1920]{2,1,0:T(8,128)(2,1)} %bitcast.97), calls=%async_computation.3 | async-start | bytes 983040 | tf_op jit(solution)/shard_map/all_to_all | solution.py:37
  138.7 2.9 %copy-start.1 = (bf16[4,128,1792]{1,2,0:T(8,128)(2,1)S(1)}, bf16[4,128,1792]{1,2,0:T(8,128)(2,1)}, u32[]{:S(2)}) copy-start(bf16[4,128,1792]{1,2,0:T(8,128)(2,1)} %copy.57) | copy-start | bytes 5505028
  138.7 2.9 %copy-start.8 = (f32[128,256]{1,0:T(8,128)S(1)}, f32[128,256]{1,0:T(8,128)}, u32[]{:S(2)}) copy-start(f32[128,256]{1,0:T(8,128)} %copy-done.7) | copy-start | bytes 393220
  138.7 2.9 %copy-start.9 = (f32[128,256]{1,0:T(8,128)S(1)}, f32[128,256]{1,0:T(8,128)}, u32[]{:S(2)}) copy-start(f32[128,256]{1,0:T(8,128)} %get-tuple-element.8) | copy-start | bytes 393220
Sparse Core Ops, SparseCore 0:
  30.2 20.0 all-gather.3
  52.5 21.1 all-gather.5
  99.5 30.6 reduce-scatter.1

commit v2 on v1

--- a/solution.py
+++ b/solution.py
@@ -43,16 +43,29 @@
         whole = lax.all_gather(shares, "dp", axis=0)
         return whole.transpose(1, 0, 2).reshape(slots, width_full)
 
+    def hop(sent, distance):
+        return lax.ppermute(sent, "dp", [(i, i ^ distance) for i in range(groups)])
+
+    def join_direct(share, far):
+        whole = jnp.zeros((groups, slots, width), share.dtype)
+        for k, chunk in enumerate([share] + far):
+            whole = lax.dynamic_update_index_in_dim(whole, chunk, part ^ (2 * k), 0)
+            whole = lax.dynamic_update_index_in_dim(whole, hop(chunk, 1), part ^ (2 * k + 1), 0)
+        return whole.transpose(1, 0, 2).reshape(slots, width_full)
+
     expert_in = join(swap(fill(tokens)))
     weight_lanes = jnp.pad(gate_slots[:, None], ((0, 0), (0, LANES - 1)))
     recv_grad = swap(jnp.concatenate([fill(grad_out), weight_lanes], axis=1))
-    expert_grad = join(recv_grad[:, :width])
+    grad_share = recv_grad[:, :width]
+    grad_far = [hop(grad_share, 2 * k) for k in range(1, groups // 2)]
     weight_col = recv_grad[:, width : width + 1].astype(jnp.float32)
     gate_mat = w_gate[0]
     up_mat = w_up[0]
     down_mat = w_down[0]
     pre_gate = jnp.dot(expert_in, gate_mat, preferred_element_type=jnp.float32)
     pre_up = jnp.dot(expert_in, up_mat, preferred_element_type=jnp.float32)
+    pre_gate, pre_up, grad_far = lax.optimization_barrier((pre_gate, pre_up, grad_far))
+    expert_grad = join_direct(grad_share, grad_far)
     sigmoid_gate = jax.nn.sigmoid(pre_gate)
     activated = pre_gate * sigmoid_gate
     hidden = activated * pre_up
@@ -78,14 +91,30 @@
     low = (gate_terms - high.astype(jnp.float32)).astype(jnp.bfloat16)
     term_lanes = jnp.pad(jnp.stack([high, low], axis=1), ((0, 0), (0, LANES - 2)))
 
-    def block(n):
-        rows = slice(n * width, (n + 1) * width)
-        first = lax.dot_general(d_gate, gate_mat[rows], CONTRACT_LAST, preferred_element_type=jnp.float32)
-        second = lax.dot_general(d_up, up_mat[rows], CONTRACT_LAST, preferred_element_type=jnp.float32)
+    def block(owner):
+        first = lax.dot_general(
+            d_gate,
+            lax.dynamic_slice_in_dim(gate_mat, owner * width, width, axis=0),
+            CONTRACT_LAST,
+            preferred_element_type=jnp.float32,
+        )
+        second = lax.dot_general(
+            d_up,
+            lax.dynamic_slice_in_dim(up_mat, owner * width, width, axis=0),
+            CONTRACT_LAST,
+            preferred_element_type=jnp.float32,
+        )
         return jnp.concatenate([(first + second).astype(jnp.bfloat16), term_lanes], axis=1)
 
-    blocks = jnp.concatenate([block(n) for n in range(groups)], axis=0)
-    summed = lax.psum_scatter(blocks, "dp", scatter_dimension=0, tiled=True)
+    def pair_sum(k):
+        arrived = hop(block(part ^ (2 * k + 1)), 1)
+        return arrived.astype(jnp.float32) + block(part ^ (2 * k)).astype(jnp.float32)
+
+    arrivals = [hop(pair_sum(k).astype(jnp.bfloat16), 2 * k) for k in range(1, groups // 2)]
+    total = pair_sum(0)
+    for arrived in arrivals:
+        total = total + arrived.astype(jnp.float32)
+    summed = total.astype(jnp.bfloat16)
     back_home = swap(summed)
     token_grad = lax.dot_general(
         place, back_home[:, :width], CONTRACT_FIRST, preferred_element_type=jnp.float32

time: 158 us -> 121 us (0.77)
  waiting for transfers between devices: 53.4 us -> 17 us
  other arithmetic: 8.66 us -> 3.86 us
  local copies, waits for them, and re-layouts: 9.63 us -> 13.5 us
  matrix products: 29.2 us -> 26.9 us
  starting transfers between devices: 5.74 us -> 7.42 us
    reduce_scatter x1 -> x0, waiting for transfers between devices: 30.8 us -> none  [on_device(): summed = lax.psum_scatter(blocks, 'dp', scatter_dimension=0, tiled=True)]
    all_gather x2 -> x1, waiting for transfers between devices: 17.7 us -> 0.02 us  [join(): whole = lax.all_gather(shares, 'dp', axis=0)]
    ppermute x0 -> x6, waiting for transfers between devices: none -> 13.8 us  [hop(): return lax.ppermute(sent, 'dp', [(i, i ^ distance) for i in range(groups)])]
    concatenate x1, other arithmetic: 5.44 us -> 0.07 us  [block(): jnp.concatenate([(first + second).astype(jnp.bfloat16), term_lanes], axis=1)]
    broadcast_in_dim x0 -> x5, local copies, waits for them, and re-layouts: none -> 4.53 us  [the longest x2 1.53 us: join_direct(): lax.dynamic_update_index_in_dim(whole, hop(chunk, 1), part ^ 2 * k + 1, 0)]
    all_gather x2 -> x1, local copies, waits for them, and re-layouts: 6.71 us -> 2.9 us  [join(): whole = lax.all_gather(shares, 'dp', axis=0)]
    ppermute x0 -> x6, starting transfers between devices: none -> 3.78 us  [hop(): return lax.ppermute(sent, 'dp', [(i, i ^ distance) for i in range(groups)])]
    dot_general x8, matrix products: 9.5 us -> 6.19 us  [the longest x4 4.33 us: block(): lax.dot_general(d_gate, lax.dynamic_slice_in_dim(gate_mat, owner * width,...]
  transfers between devices with their start and end apart: 4 -> 8, of which waited for: 4 -> 4; matrix products, arithmetic and copies ran while one was open for 11% -> 23% of each run, Pallas kernels for 0% -> 0%
where the time goes in v2:
time: 121 us; the launch traced here: 120 us
  blocking collectives  37.2 us (31%)
  matrix products  26.9 us (22%)
  waiting for transfers between devices  17 us (14%)
  between operations  14.2 us (12%)
  local copies, waits for them, and re-layouts  13.5 us (11%)
  starting transfers between devices  7.42 us (6%)
  other arithmetic  3.86 us (3%)
    all_to_all x2, blocking collectives, swap(): lax.all_to_all(sent.reshape(experts, room, sent.shape[1]), 'expert', spli...  37.2 us
    ppermute x6, waiting for transfers between devices, hop(): return lax.ppermute(sent, 'dp', [(i, i ^ distance) for i in range(groups)])  13.8 us
    dot_general x1, matrix products, on_device(): lax.dot_general(scaled, expert_grad, CONTRACT_FIRST, preferred_element_ty...  4.55 us
    dot_general x4, matrix products, block(): lax.dot_general(d_gate, lax.dynamic_slice_in_dim(gate_mat, owner * width,...  4.33 us
    dot_general x1, matrix products, on_device(): lax.dot_general(expert_grad, down_mat, CONTRACT_LAST, preferred_element_t...  4.03 us
    ppermute x6, starting transfers between devices, hop(): return lax.ppermute(sent, 'dp', [(i, i ^ distance) for i in range(groups)])  3.78 us
    all_to_all x1, starting transfers between devices, swap(): lax.all_to_all(sent.reshape(experts, room, sent.shape[1]), 'expert', spli...  3.61 us
    all_to_all x1, waiting for transfers between devices, swap(): lax.all_to_all(sent.reshape(experts, room, sent.shape[1]), 'expert', spli...  3.2 us
  transfers between devices with their start and end apart: 8, of which 4 were waited for; matrix products, arithmetic and copies ran while one was open for 23% of the time, Pallas kernels for 0%

profile of v2, /device:TPU:0, one launch (start us, length us, event | category | flops | bytes accessed | tf_op | source)
XLA Modules:
  0.0 120.1 jit_solution(17236656251880616619)
XLA Ops:
  9.7 20.4 %all_to_all.15 = bf16[8,16,1792]{2,1,0:T(8,128)(2,1)} all-to-all(bf16[8,16,1792]{2,1,0:T(8,128)(2,1)S(1)} %bitcast.98), channel_id=1, replica_groups=mesh['dp'=4,'expert'=8] {'expert'}, dimensions={0} | all-to-all | bytes 917504 | tf_op jit(solution)/shard_map/all_to_all | solution.py:37
  31.0 1.3 %convolution_convert_fusion.4 = bf16[128,1792]{1,0:T(8,128)(2,1)S(1)} fusion(pred[128,48]{0,1:T(8,128)(4,1)S(1)} %fusion.46, bf16[48,7168]{1,0:T(8,128)(2,1)} %param.8, s32[]{:T(128)S(6)} %select_n.39), kind=kOutput, calls=%fused_computation.21 | convolution fusion | flops 22249472 | bytes 636932 | tf_op jit(solution)/shard_map/dot_general | solution.py:34
  32.3 16.8 %all_to_all.16 = bf16[8,16,1920]{2,1,0:T(8,128)(2,1)S(1)} all-to-all(bf16[8,16,1920]{2,1,0:T(8,128)(2,1)S(1)} %bitcast.93), channel_id=1, replica_groups=mesh['dp'=4,'expert'=8] {'expert'}, dimensions={0} | all-to-all | bytes 983040 | tf_op jit(solution)/shard_map/all_to_all | solution.py:37
  50.0 1.5 %collective-permute-start.1 = (bf16[128,1792]{1,0:T(8,128)(2,1)}, bf16[128,1792]{1,0:T(8,128)(2,1)}, u32[]{:S(2)}, u32[]{:S(2)}) collective-permute-start(bf16[128,1792]{1,0:T(8,128)(2,1)} %get-tuple-element.11), channel_id=1, source_target_pairs={{0,16},{8,24},{16,0},{24,8},{1,17},{9,25},{17,1},{25,9},{2,18},{10... | collective-permute-start | bytes 1376264 | tf_op jit(solution)/shard_map/ppermute | solution.py:47
  51.9 1.5 %broadcast_in_dim.55 = bf16[4,128,1792]{1,2,0:T(8,128)(2,1)} broadcast(bf16[]{:T(256)} %constant.41.clone.1), dimensions={} | broadcast | bytes 1835010 | tf_op jit(solution)/shard_map/broadcast_in_dim | solution.py:50
  54.4 2.9 %copy.67 = bf16[4,128,1792]{1,2,0:T(8,128)(2,1)S(1)} copy(bf16[4,128,1792]{2,1,0:T(8,128)(2,1)} %all-gather.2.cloned.1.call-done) | data formatting | bytes 3670016 | tf_op jit(solution)/shard_map/all_gather | solution.py:43
  57.4 2.9 %fusion.5 = f32[128,256]{1,0:T(8,128)S(1)} fusion(bf16[128,7168]{0,1:T(8,128)(2,1)S(1)} %bitcast.87, bf16[1,7168,256]{2,1,0:T(8,128)(2,1)} %param.12), kind=kOutput, calls=%fused_computation.8 | convolution fusion | flops 469762048 | bytes 5636096 | tf_op jit(solution)/shard_map/dot_general | solution.py:66
  61.3 1.9 %collective-permute-done.1 = bf16[128,1792]{1,0:T(8,128)(2,1)} collective-permute-done((bf16[128,1792]{1,0:T(8,128)(2,1)}, bf16[128,1792]{1,0:T(8,128)(2,1)}, u32[]{:S(2)}, u32[]{:S(2)}) %collective-permute-start.1) | collective-permute-done | bytes 458784 | tf_op jit(solution)/shard_map/ppermute | solution.py:47
  64.0 1.3 %copy.68 = bf16[1,128,1792]{1,2,0:T(8,128)(2,1)S(1)} copy(bf16[1,128,1792]{2,1,0:T(8,128)(2,1)} %bitcast.12) | data formatting | bytes 917504 | tf_op jit(solution)/shard_map/jit(dynamic_update_index_in_dim)/broadcast_in_dim | solution.py:52
  65.3 0.8 constant_dynamic-update-slice_fusion.1
  66.1 1.3 %copy.69 = bf16[1,128,1792]{1,2,0:T(8,128)(2,1)S(1)} copy(bf16[1,128,1792]{2,1,0:T(8,128)(2,1)} %bitcast.13) | data formatting | bytes 917504 | tf_op jit(solution)/shard_map/jit(dynamic_update_index_in_dim)/broadcast_in_dim | solution.py:53
  68.2 4.0 %multiply_convert_fusion.2 = (bf16[128,256]{1,0:T(8,128)(2,1)S(1)}, f32[128]{0:T(128)S(1)}, bf16[128,256]{1,0:T(8,128)(2,1)S(1)}) fusion(f32[128,256]{1,0:T(8,128)S(1)} %fusion.7, f32[128,256]{1,0:T(8,128)S(1)} %fusion.5, f32[128]{0:T(128)S(1)} %convert_reduce_fusion, bf16[128,7168]{0,1:T(8,128)(2,1)} %bitcast.15, bf16[1,256,7168]{2,1,0:T(8,128)(2,1)} %param.13), kind=kOutput, calls=%fused_computation.59 | convolution fusion | flops 470384512 | bytes 5899264 | tf_op jit(solution)/shard_map/dot_general | solution.py:73
  72.4 1.8 %fusion.19 = f32[128,1792]{1,0:T(8,128)S(1)} fusion(bf16[128,256]{1,0:T(8,128)(2,1)S(1)} %get-tuple-element.13, bf16[1,7168,256]{2,1,0:T(8,128)(2,1)} %param.11, s32[]{:T(128)S(6)} %select_n.46), kind=kOutput, calls=%fused_computation.32 | convolution fusion | flops 117440512 | bytes 1900548 | tf_op jit(solution)/shard_map/dot_general | solution.py:95
  74.2 1.6 %fusion.25 = f32[128,1792]{1,0:T(8,128)S(1)} fusion(bf16[128,256]{1,0:T(8,128)(2,1)S(1)} %get-tuple-element.13, bf16[1,7168,256]{2,1,0:T(8,128)(2,1)} %param.11, s32[]{:T(128)S(6)} %select_n.45), kind=kOutput, calls=%fused_computation.38 | convolution fusion | flops 117440512 | bytes 1900548 | tf_op jit(solution)/shard_map/dot_general | solution.py:95
  78.8 0.8 collective-permute-done.4
  79.8 1.6 %collective-permute-start.5 = (bf16[128,1920]{1,0:T(8,128)(2,1)S(1)}, bf16[128,1920]{1,0:T(8,128)(2,1)S(1)}, u32[]{:S(2)}, u32[]{:S(2)}) collective-permute-start(bf16[128,1920]{1,0:T(8,128)(2,1)S(1)} %add_convert_fusion.1), channel_id=1, source_target_pairs={{0,16},{8,24},{16,0},{24,8},{1,17},{9,25},{17,1},{25,9},{2,18},{10... | collective-permute-start | bytes 1474568 | tf_op jit(solution)/shard_map/ppermute | solution.py:47
  82.3 11.0 %collective-permute-done.5 = bf16[128,1920]{1,0:T(8,128)(2,1)S(1)} collective-permute-done((bf16[128,1920]{1,0:T(8,128)(2,1)S(1)}, bf16[128,1920]{1,0:T(8,128)(2,1)S(1)}, u32[]{:S(2)}, u32[]{:S(2)}) %collective-permute-start.5) | collective-permute-done | bytes 491552 | tf_op jit(solution)/shard_map/ppermute | solution.py:47
  93.3 1.0 add_convert_fusion
  94.3 3.6 %all-to-all-start.2 = ((bf16[8,16,1920]{2,1,0:T(8,128)(2,1)}), bf16[8,16,1920]{2,1,0:T(8,128)(2,1)S(1)}, u32[]{:S(2)}, u32[]{:S(2)}) async-start(bf16[8,16,1920]{2,1,0:T(8,128)(2,1)} %bitcast.96), calls=%async_computation.2 | async-start | bytes 983040 | tf_op jit(solution)/shard_map/all_to_all | solution.py:37
  97.9 2.9 %fusion.1 = bf16[1,7168,256]{2,1,0:T(8,128)(2,1)} fusion(bf16[128,7168]{0,1:T(8,128)(2,1)S(1)} %bitcast.89, bf16[128,256]{1,0:T(8,128)(2,1)S(1)} %get-tuple-element.15), kind=kOutput, calls=%fused_computation.4 | convolution fusion | flops 471597056 | bytes 5570560 | tf_op jit(solution)/shard_map/dot_general | solution.py:87
  100.8 2.9 %fusion = bf16[1,7168,256]{2,1,0:T(8,128)(2,1)} fusion(bf16[128,7168]{0,1:T(8,128)(2,1)S(1)} %bitcast.90, bf16[128,256]{1,0:T(8,128)(2,1)S(1)} %get-tuple-element.13), kind=kOutput, calls=%fused_computation.3 | convolution fusion | flops 471597056 | bytes 5570560 | tf_op jit(solution)/shard_map/dot_general | solution.py:84
  103.8 4.5 %fusion.2 = bf16[1,256,7168]{2,1,0:T(8,128)(2,1)} fusion(bf16[128,7168]{0,1:T(8,128)(2,1)} %bitcast.15, f32[128]{0:T(128)S(1)} %convert_reduce_fusion, f32[128,256]{1,0:T(8,128)S(1)} %fusion.5, f32[128,256]{1,0:T(8,128)S(1)} %fusion.7), kind=kOutput, calls=%fused_computation.5 | convolution fusion | flops 471826432 | bytes 5767680 | tf_op jit(solution)/shard_map/dot_general | solution.py:76
  108.3 3.2 %all-to-all-done.2 = bf16[8,16,1920]{2,1,0:T(8,128)(2,1)S(1)} async-done(((bf16[8,16,1920]{2,1,0:T(8,128)(2,1)}), bf16[8,16,1920]{2,1,0:T(8,128)(2,1)S(1)}, u32[]{:S(2)}, u32[]{:S(2)}) %all-to-all-start.2) | async-done | bytes 491552 | tf_op jit(solution)/shard_map/all_to_all | solution.py:37
  111.6 0.9 convolution_convert_fusion.5
  (52 shorter events, 13.3 us)
Async XLA Ops:
  7.2 2.2 %copy-start = (bf16[48,7168]{1,0:T(8,128)(2,1)S(1)}, bf16[48,7168]{1,0:T(8,128)(2,1)}, u32[]{:S(2)}) copy-start(bf16[48,7168]{1,0:T(8,128)(2,1)} %param.7) | copy-start | bytes 2064388
  7.2 47.2 %all-gather.2.cloned.1.call-start = ((), (), s32[]{:S(2)}) async-start(), calls=%async_computation.3 | async-start | bytes 2293760 | tf_op jit(solution)/shard_map/all_gather | solution.py:43
  50.0 4.2 %collective-permute-start = (bf16[128,1792]{1,0:T(8,128)(2,1)}, bf16[128,1792]{1,0:T(8,128)(2,1)S(1)}, u32[]{:S(2)}, u32[]{:S(2)}) collective-permute-start(bf16[128,1792]{1,0:T(8,128)(2,1)} %get-tuple-element.11), channel_id=1, source_target_pairs={{0,8},{8,0},{16,24},{24,16},{1,9},{9,1},{17,25},{25,17},{2,10},{10... | collective-permute-start | bytes 1376264 | tf_op jit(solution)/shard_map/ppermute | solution.py:47
  50.0 13.2 %collective-permute-start.1 = (bf16[128,1792]{1,0:T(8,128)(2,1)}, bf16[128,1792]{1,0:T(8,128)(2,1)}, u32[]{:S(2)}, u32[]{:S(2)}) collective-permute-start(bf16[128,1792]{1,0:T(8,128)(2,1)} %get-tuple-element.11), channel_id=1, source_target_pairs={{0,16},{8,24},{16,0},{24,8},{1,17},{9,25},{17,1},{25,9},{2,18},{10... | collective-permute-start | bytes 1376264 | tf_op jit(solution)/shard_map/ppermute | solution.py:47
  57.3 3.1 %copy-start.2 = (bf16[1,7168,256]{2,1,0:T(8,128)(2,1)S(1)}, bf16[1,7168,256]{2,1,0:T(8,128)(2,1)}, u32[]{:S(2)}) copy-start(bf16[1,7168,256]{2,1,0:T(8,128)(2,1)} %param.11) | copy-start | bytes 11010052
  63.2 2.9 %collective-permute-start.2 = (bf16[128,1792]{1,0:T(8,128)(2,1)}, bf16[128,1792]{1,0:T(8,128)(2,1)}, u32[]{:S(2)}, u32[]{:S(2)}) collective-permute-start(bf16[128,1792]{1,0:T(8,128)(2,1)} %collective-permute-done.1), channel_id=1, source_target_pairs={{0,8},{8,0},{16,24},{24,16},{1,9},{9,1},{17,25},{25,17},{2,10},{10... | collective-permute-start | bytes 1376264 | tf_op jit(solution)/shard_map/ppermute | solution.py:47
  72.4 3.4 %copy-start.1 = (bf16[1,7168,256]{2,1,0:T(8,128)(2,1)S(1)}, bf16[1,7168,256]{2,1,0:T(8,128)(2,1)}, u32[]{:S(2)}) copy-start(bf16[1,7168,256]{2,1,0:T(8,128)(2,1)} %param.12) | copy-start | bytes 11010052
  75.8 2.0 %copy-start.3 = (bf16[1,7168,256]{2,1,0:T(8,128)(2,1)S(1)}, bf16[1,7168,256]{2,1,0:T(8,128)(2,1)}, u32[]{:S(2)}) copy-start(bf16[1,7168,256]{2,1,0:T(8,128)(2,1)} %param.11) | copy-start | bytes 11010052
  76.9 5.4 %collective-permute-start.3 = (bf16[128,1920]{1,0:T(8,128)(2,1)S(1)}, bf16[128,1920]{1,0:T(8,128)(2,1)S(1)}, u32[]{:S(2)}, u32[]{:S(2)}) collective-permute-start(bf16[128,1920]{1,0:T(8,128)(2,1)S(1)} %get-tuple-element.16), channel_id=1, source_target_pairs={{0,8},{8,0},{16,24},{24,16},{1,9},{9,1},{17,25},{25,17},{2,10},{10... | collective-permute-start | bytes 1474568 | tf_op jit(solution)/shard_map/ppermute | solution.py:47
  77.5 2.2 %collective-permute-start.4 = (bf16[128,1920]{1,0:T(8,128)(2,1)S(1)}, bf16[128,1920]{1,0:T(8,128)(2,1)S(1)}, u32[]{:S(2)}, u32[]{:S(2)}) collective-permute-start(bf16[128,1920]{1,0:T(8,128)(2,1)S(1)} %get-tuple-element.17), channel_id=1, source_target_pairs={{0,8},{8,0},{16,24},{24,16},{1,9},{9,1},{17,25},{25,17},{2,10},{10... | collective-permute-start | bytes 1474568 | tf_op jit(solution)/shard_map/ppermute | solution.py:47
  79.8 13.6 %collective-permute-start.5 = (bf16[128,1920]{1,0:T(8,128)(2,1)S(1)}, bf16[128,1920]{1,0:T(8,128)(2,1)S(1)}, u32[]{:S(2)}, u32[]{:S(2)}) collective-permute-start(bf16[128,1920]{1,0:T(8,128)(2,1)S(1)} %add_convert_fusion.1), channel_id=1, source_target_pairs={{0,16},{8,24},{16,0},{24,8},{1,17},{9,25},{17,1},{25,9},{2,18},{10... | collective-permute-start | bytes 1474568 | tf_op jit(solution)/shard_map/ppermute | solution.py:47
  94.3 17.2 %all-to-all-start.2 = ((bf16[8,16,1920]{2,1,0:T(8,128)(2,1)}), bf16[8,16,1920]{2,1,0:T(8,128)(2,1)S(1)}, u32[]{:S(2)}, u32[]{:S(2)}) async-start(bf16[8,16,1920]{2,1,0:T(8,128)(2,1)} %bitcast.96), calls=%async_computation.2 | async-start | bytes 983040 | tf_op jit(solution)/shard_map/all_to_all | solution.py:37
Sparse Core Ops, SparseCore 0:
  30.2 20.0 all-gather.1

commit v3 on v2

--- a/solution.py
+++ b/solution.py
@@ -47,11 +47,16 @@
         return lax.ppermute(sent, "dp", [(i, i ^ distance) for i in range(groups)])
 
     def join_direct(share, far):
-        whole = jnp.zeros((groups, slots, width), share.dtype)
-        for k, chunk in enumerate([share] + far):
-            whole = lax.dynamic_update_index_in_dim(whole, chunk, part ^ (2 * k), 0)
-            whole = lax.dynamic_update_index_in_dim(whole, hop(chunk, 1), part ^ (2 * k + 1), 0)
-        return whole.transpose(1, 0, 2).reshape(slots, width_full)
+        chunks = []
+        for chunk in [share] + far:
+            chunks += [chunk, hop(chunk, 1)]
+        ordered = []
+        for n in range(groups):
+            picked = chunks[0]
+            for k in range(1, groups):
+                picked = jnp.where(part == n ^ k, chunks[k], picked)
+            ordered.append(picked)
+        return jnp.concatenate(ordered, axis=1)
 
     expert_in = join(swap(fill(tokens)))
     weight_lanes = jnp.pad(gate_slots[:, None], ((0, 0), (0, LANES - 1)))
@@ -91,9 +96,9 @@
     low = (gate_terms - high.astype(jnp.float32)).astype(jnp.bfloat16)
     term_lanes = jnp.pad(jnp.stack([high, low], axis=1), ((0, 0), (0, LANES - 2)))
 
-    def block(owner):
+    def block(owner, gate_side):
         first = lax.dot_general(
-            d_gate,
+            gate_side,
             lax.dynamic_slice_in_dim(gate_mat, owner * width, width, axis=0),
             CONTRACT_LAST,
             preferred_element_type=jnp.float32,
@@ -106,12 +111,19 @@
         )
         return jnp.concatenate([(first + second).astype(jnp.bfloat16), term_lanes], axis=1)
 
-    def pair_sum(k):
-        arrived = hop(block(part ^ (2 * k + 1)), 1)
-        return arrived.astype(jnp.float32) + block(part ^ (2 * k)).astype(jnp.float32)
-
-    arrivals = [hop(pair_sum(k).astype(jnp.bfloat16), 2 * k) for k in range(1, groups // 2)]
-    total = pair_sum(0)
+    gate_side = d_gate
+    arrivals = []
+    for k in list(range(1, groups // 2)) + [0]:
+        leaving = block(part ^ (2 * k + 1), gate_side)
+        leaving, gate_side = lax.optimization_barrier((leaving, gate_side))
+        arrived = hop(leaving, 1)
+        kept = block(part ^ (2 * k), gate_side)
+        pair = arrived.astype(jnp.float32) + kept.astype(jnp.float32)
+        if k:
+            pair, gate_side = lax.optimization_barrier((pair.astype(jnp.bfloat16), gate_side))
+            arrivals.append(hop(pair, 2 * k))
+        else:
+            total = pair
     for arrived in arrivals:
         total = total + arrived.astype(jnp.float32)
     summed = total.astype(jnp.bfloat16)

time: 121 us -> 118 us (0.975)
  local copies, waits for them, and re-layouts: 13.5 us -> 5.93 us
  matrix products: 26.9 us -> 28.7 us
  waiting for transfers between devices: 17 us -> 18.8 us
  other arithmetic: 3.86 us -> 5.37 us
    broadcast_in_dim x5 -> x0, local copies, waits for them, and re-layouts: 4.53 us -> none  [the longest x2 1.53 us: join_direct(): lax.dynamic_update_index_in_dim(whole, hop(chunk, 1), part ^ 2 * k + 1, 0)]
    dynamic_update_slice x4 -> x0, local copies, waits for them, and re-layouts: 3.24 us -> none  [the longest x2 1.63 us: join_direct(): whole = lax.dynamic_update_index_in_dim(whole, chunk, part ^ 2 * k, 0)]
    select_n x0 -> x1, other arithmetic: none -> 1.51 us  [join_direct(): picked = jnp.where(part == n ^ k, chunks[k], picked)]
    dot_general x1, matrix products: 4.55 us -> 3.05 us  [on_device(): lax.dot_general(scaled, expert_grad, CONTRACT_FIRST, preferred_element_ty...]
  transfers between devices with their start and end apart: 8 -> 8, of which waited for: 4 -> 4; matrix products, arithmetic and copies ran while one was open for 23% -> 21% of each run, Pallas kernels for 0% -> 0%
where the time goes in v3:
time: 118 us
  blocking collectives  37.2 us (32%)
  matrix products  28.7 us (24%)
  waiting for transfers between devices  18.8 us (16%)
  between operations  14.3 us (12%)
  starting transfers between devices  7.25 us (6%)
  local copies, waits for them, and re-layouts  5.93 us (5%)
  other arithmetic  5.37 us (5%)
    all_to_all x2, blocking collectives, swap(): lax.all_to_all(sent.reshape(experts, room, sent.shape[1]), 'expert', spli...  37.2 us
    ppermute x6, waiting for transfers between devices, hop(): return lax.ppermute(sent, 'dp', [(i, i ^ distance) for i in range(groups)])  14.9 us
    dot_general x4, matrix products, block(): lax.dot_general(gate_side, lax.dynamic_slice_in_dim(gate_mat, owner * wid...  4.47 us
    dot_general x1, matrix products, on_device(): lax.dot_general(expert_grad, down_mat, CONTRACT_LAST, preferred_element_t...  3.9 us
    all_to_all x1, waiting for transfers between devices, swap(): lax.all_to_all(sent.reshape(experts, room, sent.shape[1]), 'expert', spli...  3.88 us
    dot_general x1, matrix products, on_device(): lax.dot_general(expert_in, d_up, CONTRACT_FIRST, preferred_element_type=j...  3.78 us
    all_to_all x1, starting transfers between devices, swap(): lax.all_to_all(sent.reshape(experts, room, sent.shape[1]), 'expert', spli...  3.62 us
    dot_general x1, matrix products, on_device(): pre_up = jnp.dot(expert_in, up_mat, preferred_element_type=jnp.float32)  3.6 us
  transfers between devices with their start and end apart: 8, of which 4 were waited for; matrix products, arithmetic and copies ran while one was open for 21% of the time, Pallas kernels for 0%

profile of v3, /device:TPU:0, one launch (start us, length us, event | category | flops | bytes accessed | tf_op | source)
XLA Modules:
  0.0 117.6 jit_solution(6530127968020776426)
XLA Ops:
  7.2 0.8 copy.50
  9.7 20.4 %all_to_all.15 = bf16[8,16,1792]{2,1,0:T(8,128)(2,1)} all-to-all(bf16[8,16,1792]{2,1,0:T(8,128)(2,1)S(1)} %bitcast.88), channel_id=1, replica_groups=mesh['dp'=4,'expert'=8] {'expert'}, dimensions={0} | all-to-all | bytes 917504 | tf_op jit(solution)/shard_map/all_to_all | solution.py:37
  31.0 1.3 %convolution_convert_fusion.4 = bf16[128,1792]{1,0:T(8,128)(2,1)S(1)} fusion(pred[128,48]{0,1:T(8,128)(4,1)S(1)} %fusion.46, bf16[48,7168]{1,0:T(8,128)(2,1)} %param.8, s32[]{:T(128)S(6)} %select_n.84), kind=kOutput, calls=%fused_computation.21 | convolution fusion | flops 22249472 | bytes 636932 | tf_op jit(solution)/shard_map/dot_general | solution.py:34
  32.3 16.8 %all_to_all.16 = bf16[8,16,1920]{2,1,0:T(8,128)(2,1)S(1)} all-to-all(bf16[8,16,1920]{2,1,0:T(8,128)(2,1)S(1)} %bitcast.86), channel_id=1, replica_groups=mesh['dp'=4,'expert'=8] {'expert'}, dimensions={0} | all-to-all | bytes 983040 | tf_op jit(solution)/shard_map/all_to_all | solution.py:37
  49.9 1.5 %collective-permute-start = (bf16[128,1792]{1,0:T(8,128)(2,1)}, bf16[128,1792]{1,0:T(8,128)(2,1)}, u32[]{:S(2)}, u32[]{:S(2)}) collective-permute-start(bf16[128,1792]{1,0:T(8,128)(2,1)} %slice.17), channel_id=1, source_target_pairs={{0,16},{8,24},{16,0},{24,8},{1,17},{9,25},{17,1},{25,9},{2,18},{10... | collective-permute-start | bytes 1376264 | tf_op jit(solution)/shard_map/ppermute | solution.py:47
  51.5 2.9 %copy.53 = bf16[4,128,1792]{1,2,0:T(8,128)(2,1)S(1)} copy(bf16[4,128,1792]{2,1,0:T(8,128)(2,1)} %all-gather.2.cloned.1.call-done) | data formatting | bytes 3670016 | tf_op jit(solution)/shard_map/all_gather | solution.py:43
  54.4 3.6 %fusion.5 = f32[128,256]{1,0:T(8,128)} fusion(bf16[128,7168]{0,1:T(8,128)(2,1)S(1)} %bitcast.77, bf16[1,7168,256]{2,1,0:T(8,128)(2,1)} %param.12), kind=kOutput, calls=%fused_computation.8 | convolution fusion | flops 469762048 | bytes 5636096 | tf_op jit(solution)/shard_map/dot_general | solution.py:71
  58.0 1.5 %fusion.7 = f32[128,256]{1,0:T(8,128)} fusion(bf16[128,7168]{0,1:T(8,128)(2,1)S(1)} %bitcast.78, bf16[1,7168,256]{2,1,0:T(8,128)(2,1)S(1)} %copy-done.2), kind=kOutput, calls=%fused_computation.10 | convolution fusion | flops 469762048 | bytes 5636096 | tf_op jit(solution)/shard_map/dot_general | solution.py:70
  59.4 3.7 %collective-permute-done = bf16[128,1792]{1,0:T(8,128)(2,1)} collective-permute-done((bf16[128,1792]{1,0:T(8,128)(2,1)}, bf16[128,1792]{1,0:T(8,128)(2,1)}, u32[]{:S(2)}, u32[]{:S(2)}) %collective-permute-start) | collective-permute-done | bytes 458784 | tf_op jit(solution)/shard_map/ppermute | solution.py:47
  64.1 1.3 %collective-permute-done.1 = bf16[128,1792]{1,0:T(8,128)(2,1)} collective-permute-done((bf16[128,1792]{1,0:T(8,128)(2,1)}, bf16[128,1792]{1,0:T(8,128)(2,1)}, u32[]{:S(2)}, u32[]{:S(2)}) %collective-permute-start.1) | collective-permute-done | bytes 458784 | tf_op jit(solution)/shard_map/ppermute | solution.py:47
  65.4 1.5 %select_select_fusion.3 = (bf16[128,1792]{1,0:T(8,128)(2,1)S(1)}, bf16[128,1792]{1,0:T(8,128)(2,1)S(1)}, bf16[128,1792]{1,0:T(8,128)(2,1)S(1)}, bf16[128,1792]{1,0:T(8,128)(2,1)S(1)}) fusion(bf16[128,1792]{1,0:T(8,128)(2,1)} %collective-permute-done.1, bf16[128,1792]{1,0:T(8,128)(2,1)} %collective-permute-done, bf16[128,1792]{1,0:T(8,128)(2,1)} %copy-done.15, ...), kind=kLoop, calls=%fused_computation.58 | loop fusion | flops 2752512 | bytes 3670020 | tf_op jit(solution)/shard_map/jit(_where)/select_n | solution.py:57
  66.9 3.9 %multiply_convert_fusion.2 = (bf16[128,256]{1,0:T(8,128)(2,1)S(1)}, f32[128]{0:T(128)S(1)}, bf16[128,256]{1,0:T(8,128)(2,1)S(1)}) fusion(f32[128,256]{1,0:T(8,128)S(1)} %copy-done.13, f32[128,256]{1,0:T(8,128)S(1)} %copy-done.11, f32[128]{0:T(128)S(1)} %convert_reduce_fusion, bf16[1,256,7168]{2,1,0:T(8,128)(2,1)} %param.13, ...), kind=kOutput, calls=%fused_computation.64 | convolution fusion | flops 477724544 | bytes 5899264 | tf_op jit(solution)/shard_map/dot_general | solution.py:78
  71.0 1.8 %fusion.25 = f32[128,1792]{1,0:T(8,128)S(1)} fusion(bf16[128,256]{1,0:T(8,128)(2,1)S(1)} %get-tuple-element.21, bf16[1,7168,256]{2,1,0:T(8,128)(2,1)} %param.11, s32[]{:T(128)S(6)} %select_n.102), kind=kOutput, calls=%fused_computation.39 | convolution fusion | flops 117440512 | bytes 1900548 | tf_op jit(solution)/shard_map/dot_general | solution.py:100
  72.8 1.6 %fusion.9 = bf16[128,1792]{1,0:T(8,128)(2,1)S(1)} fusion(f32[128,1792]{1,0:T(8,128)S(1)} %fusion.25, bf16[128,256]{1,0:T(8,128)(2,1)S(1)} %get-tuple-element.29, bf16[1,7168,256]{2,1,0:T(8,128)(2,1)} %param.12, s32[]{:T(128)S(6)} %select_n.102), kind=kOutput, calls=%fused_computation.16 | convolution fusion | flops 117899264 | bytes 2359300 | tf_op jit(solution)/shard_map/dot_general | solution.py:106
  74.7 1.8 %fusion.22 = f32[128,1792]{1,0:T(8,128)S(1)} fusion(bf16[128,256]{1,0:T(8,128)(2,1)S(1)} %get-tuple-element.21, bf16[1,7168,256]{2,1,0:T(8,128)(2,1)} %param.11, s32[]{:T(128)S(6)} %select_n.103), kind=kOutput, calls=%fused_computation.36 | convolution fusion | flops 117440512 | bytes 1900548 | tf_op jit(solution)/shard_map/dot_general | solution.py:100
  77.1 1.6 %collective-permute-start.5 = (bf16[128,1920]{1,0:T(8,128)(2,1)S(1)}, bf16[128,1920]{1,0:T(8,128)(2,1)S(1)}, u32[]{:S(2)}, u32[]{:S(2)}) collective-permute-start(bf16[128,1920]{1,0:T(8,128)(2,1)S(1)} %add_convert_fusion.1), channel_id=1, source_target_pairs={{0,16},{8,24},{16,0},{24,8},{1,17},{9,25},{17,1},{25,9},{2,18},{10... | collective-permute-start | bytes 1474568 | tf_op jit(solution)/shard_map/ppermute | solution.py:47
  80.9 9.9 %collective-permute-done.5 = bf16[128,1920]{1,0:T(8,128)(2,1)S(1)} collective-permute-done((bf16[128,1920]{1,0:T(8,128)(2,1)S(1)}, bf16[128,1920]{1,0:T(8,128)(2,1)S(1)}, u32[]{:S(2)}, u32[]{:S(2)}) %collective-permute-start.5) | collective-permute-done | bytes 491552 | tf_op jit(solution)/shard_map/ppermute | solution.py:47
  90.8 1.0 add_convert_fusion
  91.7 3.6 %all-to-all-start.2 = ((bf16[8,16,1920]{2,1,0:T(8,128)(2,1)}), bf16[8,16,1920]{2,1,0:T(8,128)(2,1)S(1)}, u32[]{:S(2)}, u32[]{:S(2)}) async-start(bf16[8,16,1920]{2,1,0:T(8,128)(2,1)} %bitcast.20), calls=%async_computation.2 | async-start | bytes 983040 | tf_op jit(solution)/shard_map/all_to_all | solution.py:37
  95.4 3.8 %fusion.1 = bf16[1,7168,256]{2,1,0:T(8,128)(2,1)} fusion(bf16[128,7168]{0,1:T(8,128)(2,1)S(1)} %bitcast.79, bf16[128,256]{1,0:T(8,128)(2,1)} %copy-done.10), kind=kOutput, calls=%fused_computation.4 | convolution fusion | flops 471597056 | bytes 5570560 | tf_op jit(solution)/shard_map/dot_general | solution.py:92
  99.2 2.9 %fusion = bf16[1,7168,256]{2,1,0:T(8,128)(2,1)} fusion(bf16[128,7168]{0,1:T(8,128)(2,1)S(1)} %bitcast.80, bf16[128,256]{1,0:T(8,128)(2,1)S(1)} %get-tuple-element.21), kind=kOutput, calls=%fused_computation.3 | convolution fusion | flops 471597056 | bytes 5570560 | tf_op jit(solution)/shard_map/dot_general | solution.py:89
  102.1 3.0 %fusion.2 = bf16[1,256,7168]{2,1,0:T(8,128)(2,1)} fusion(bf16[128,1792]{1,0:T(8,128)(2,1)S(1)} %copy-done.5, bf16[128,1792]{1,0:T(8,128)(2,1)S(1)} %copy-done.7, bf16[128,1792]{1,0:T(8,128)(2,1)S(1)} %copy-done.9, bf16[128,1792]{1,0:T(8,128)(2,1)S(1)} %get-tuple-element.23, f32[128]{0:T(128)S(1)} %convert_reduce_fusion, f32[128,256]{1,0:T(8,128)S(1)} %copy-done.12, ...), kind=kOutput, calls=%fused_computation.5 | convolution fusion | flops 479166464 | bytes 5767680 | tf_op jit(solution)/shard_map/dot_general | solution.py:81
  105.2 3.9 %all-to-all-done.2 = bf16[8,16,1920]{2,1,0:T(8,128)(2,1)S(1)} async-done(((bf16[8,16,1920]{2,1,0:T(8,128)(2,1)}), bf16[8,16,1920]{2,1,0:T(8,128)(2,1)S(1)}, u32[]{:S(2)}, u32[]{:S(2)}) %all-to-all-start.2) | async-done | bytes 491552 | tf_op jit(solution)/shard_map/all_to_all | solution.py:37
  109.2 0.9 convolution_convert_fusion.5
  (69 shorter events, 8.3 us)
Async XLA Ops:
  7.2 2.2 %copy-start = (bf16[48,7168]{1,0:T(8,128)(2,1)S(1)}, bf16[48,7168]{1,0:T(8,128)(2,1)}, u32[]{:S(2)}) copy-start(bf16[48,7168]{1,0:T(8,128)(2,1)} %param.7) | copy-start | bytes 2064388
  7.2 44.3 %all-gather.2.cloned.1.call-start = ((), (), s32[]{:S(2)}) async-start(), calls=%async_computation.3 | async-start | bytes 2293760 | tf_op jit(solution)/shard_map/all_gather | solution.py:43
  49.9 13.4 %collective-permute-start.2 = (bf16[128,1792]{1,0:T(8,128)(2,1)}, bf16[128,1792]{1,0:T(8,128)(2,1)S(1)}, u32[]{:S(2)}, u32[]{:S(2)}) collective-permute-start(bf16[128,1792]{1,0:T(8,128)(2,1)} %slice.17), channel_id=1, source_target_pairs={{0,8},{8,0},{16,24},{24,16},{1,9},{9,1},{17,25},{25,17},{2,10},{10... | collective-permute-start | bytes 1376264 | tf_op jit(solution)/shard_map/ppermute | solution.py:47
  49.9 13.2 %collective-permute-start = (bf16[128,1792]{1,0:T(8,128)(2,1)}, bf16[128,1792]{1,0:T(8,128)(2,1)}, u32[]{:S(2)}, u32[]{:S(2)}) collective-permute-start(bf16[128,1792]{1,0:T(8,128)(2,1)} %slice.17), channel_id=1, source_target_pairs={{0,16},{8,24},{16,0},{24,8},{1,17},{9,25},{17,1},{25,9},{2,18},{10... | collective-permute-start | bytes 1376264 | tf_op jit(solution)/shard_map/ppermute | solution.py:47
  54.4 3.6 %copy-start.2 = (bf16[1,7168,256]{2,1,0:T(8,128)(2,1)S(1)}, bf16[1,7168,256]{2,1,0:T(8,128)(2,1)}, u32[]{:S(2)}) copy-start(bf16[1,7168,256]{2,1,0:T(8,128)(2,1)} %param.11) | copy-start | bytes 11010052
  63.2 2.2 %collective-permute-start.1 = (bf16[128,1792]{1,0:T(8,128)(2,1)}, bf16[128,1792]{1,0:T(8,128)(2,1)}, u32[]{:S(2)}, u32[]{:S(2)}) collective-permute-start(bf16[128,1792]{1,0:T(8,128)(2,1)} %collective-permute-done), channel_id=1, source_target_pairs={{0,8},{8,0},{16,24},{24,16},{1,9},{9,1},{17,25},{25,17},{2,10},{10... | collective-permute-start | bytes 1376264 | tf_op jit(solution)/shard_map/ppermute | solution.py:47
  63.2 3.7 %copy-start.11 = (f32[128,256]{1,0:T(8,128)S(1)}, f32[128,256]{1,0:T(8,128)}, u32[]{:S(2)}) copy-start(f32[128,256]{1,0:T(8,128)} %fusion.5) | copy-start | bytes 393220
  63.2 3.7 %copy-start.13 = (f32[128,256]{1,0:T(8,128)S(1)}, f32[128,256]{1,0:T(8,128)}, u32[]{:S(2)}) copy-start(f32[128,256]{1,0:T(8,128)} %fusion.7) | copy-start | bytes 393220
  63.3 0.8 copy-start.15
  66.9 4.0 %copy-start.4 = (bf16[128,1792]{1,0:T(8,128)(2,1)}, bf16[128,1792]{1,0:T(8,128)(2,1)S(1)}, u32[]{:S(2)}) copy-start(bf16[128,1792]{1,0:T(8,128)(2,1)S(1)} %get-tuple-element.24) | copy-start | bytes 1376260
  66.9 4.0 %copy-start.6 = (bf16[128,1792]{1,0:T(8,128)(2,1)}, bf16[128,1792]{1,0:T(8,128)(2,1)S(1)}, u32[]{:S(2)}) copy-start(bf16[128,1792]{1,0:T(8,128)(2,1)S(1)} %get-tuple-element.25) | copy-start | bytes 1376260
  66.9 4.0 %copy-start.8 = (bf16[128,1792]{1,0:T(8,128)(2,1)}, bf16[128,1792]{1,0:T(8,128)(2,1)S(1)}, u32[]{:S(2)}) copy-start(bf16[128,1792]{1,0:T(8,128)(2,1)S(1)} %get-tuple-element.26) | copy-start | bytes 1376260
  70.8 9.5 %copy-start.10 = (bf16[128,256]{1,0:T(8,128)(2,1)}, bf16[128,256]{1,0:T(8,128)(2,1)S(1)}, u32[]{:S(2)}) copy-start(bf16[128,256]{1,0:T(8,128)(2,1)S(1)} %get-tuple-element.29) | copy-start | bytes 196612
  71.0 5.5 %copy-start.1 = (bf16[1,7168,256]{2,1,0:T(8,128)(2,1)S(1)}, bf16[1,7168,256]{2,1,0:T(8,128)(2,1)}, u32[]{:S(2)}) copy-start(bf16[1,7168,256]{2,1,0:T(8,128)(2,1)} %param.12) | copy-start | bytes 11010052
  74.5 4.2 %copy-start.3 = (bf16[1,7168,256]{2,1,0:T(8,128)(2,1)S(1)}, bf16[1,7168,256]{2,1,0:T(8,128)(2,1)}, u32[]{:S(2)}) copy-start(bf16[1,7168,256]{2,1,0:T(8,128)(2,1)} %param.11) | copy-start | bytes 11010052
  74.5 2.5 %collective-permute-start.3 = (bf16[128,1920]{1,0:T(8,128)(2,1)S(1)}, bf16[128,1920]{1,0:T(8,128)(2,1)S(1)}, u32[]{:S(2)}, u32[]{:S(2)}) collective-permute-start(bf16[128,1920]{1,0:T(8,128)(2,1)S(1)} %fusion.38), channel_id=1, source_target_pairs={{0,8},{8,0},{16,24},{24,16},{1,9},{9,1},{17,25},{25,17},{2,10},{10... | collective-permute-start | bytes 1474568 | tf_op jit(solution)/shard_map/ppermute | solution.py:47
  77.1 13.7 %collective-permute-start.5 = (bf16[128,1920]{1,0:T(8,128)(2,1)S(1)}, bf16[128,1920]{1,0:T(8,128)(2,1)S(1)}, u32[]{:S(2)}, u32[]{:S(2)}) collective-permute-start(bf16[128,1920]{1,0:T(8,128)(2,1)S(1)} %add_convert_fusion.1), channel_id=1, source_target_pairs={{0,16},{8,24},{16,0},{24,8},{1,17},{9,25},{17,1},{25,9},{2,18},{10... | collective-permute-start | bytes 1474568 | tf_op jit(solution)/shard_map/ppermute | solution.py:47
  79.7 11.1 %collective-permute-start.4 = (bf16[128,1920]{1,0:T(8,128)(2,1)S(1)}, bf16[128,1920]{1,0:T(8,128)(2,1)S(1)}, u32[]{:S(2)}, u32[]{:S(2)}) collective-permute-start(bf16[128,1920]{1,0:T(8,128)(2,1)S(1)} %fusion.36), channel_id=1, source_target_pairs={{0,8},{8,0},{16,24},{24,16},{1,9},{9,1},{17,25},{25,17},{2,10},{10... | collective-permute-start | bytes 1474568 | tf_op jit(solution)/shard_map/ppermute | solution.py:47
  91.7 17.3 %all-to-all-start.2 = ((bf16[8,16,1920]{2,1,0:T(8,128)(2,1)}), bf16[8,16,1920]{2,1,0:T(8,128)(2,1)S(1)}, u32[]{:S(2)}, u32[]{:S(2)}) async-start(bf16[8,16,1920]{2,1,0:T(8,128)(2,1)} %bitcast.20), calls=%async_computation.2 | async-start | bytes 983040 | tf_op jit(solution)/shard_map/all_to_all | solution.py:37
  99.1 3.0 %copy-start.5 = (bf16[128,1792]{1,0:T(8,128)(2,1)S(1)}, bf16[128,1792]{1,0:T(8,128)(2,1)}, u32[]{:S(2)}) copy-start(bf16[128,1792]{1,0:T(8,128)(2,1)} %copy-done.4) | copy-start | bytes 1376260
  99.1 3.0 %copy-start.7 = (bf16[128,1792]{1,0:T(8,128)(2,1)S(1)}, bf16[128,1792]{1,0:T(8,128)(2,1)}, u32[]{:S(2)}) copy-start(bf16[128,1792]{1,0:T(8,128)(2,1)} %copy-done.6) | copy-start | bytes 1376260
  99.1 3.0 %copy-start.9 = (bf16[128,1792]{1,0:T(8,128)(2,1)S(1)}, bf16[128,1792]{1,0:T(8,128)(2,1)}, u32[]{:S(2)}) copy-start(bf16[128,1792]{1,0:T(8,128)(2,1)} %copy-done.8) | copy-start | bytes 1376260
  99.1 3.0 %copy-start.12 = (f32[128,256]{1,0:T(8,128)S(1)}, f32[128,256]{1,0:T(8,128)}, u32[]{:S(2)}) copy-start(f32[128,256]{1,0:T(8,128)} %fusion.5) | copy-start | bytes 393220
  99.1 3.0 %copy-start.14 = (f32[128,256]{1,0:T(8,128)S(1)}, f32[128,256]{1,0:T(8,128)}, u32[]{:S(2)}) copy-start(f32[128,256]{1,0:T(8,128)} %fusion.7) | copy-start | bytes 393220
Sparse Core Ops, SparseCore 0:
  30.2 20.0 all-gather.1
